TPU v7x, 128 devices: a whole 4x4x4 slice. The times are simulated.
128 devices in a mesh: depth: 4 (over z_lo, core), row: 4 (over x), col: 8 (over z_hi, y).
Axes of the slice: x: 4, y: 4, z: 4 (z_hi: 2, z_lo: 2; z = z_hi * 2 + z_lo), core: 2. Of those that a mesh axis runs over, the one named last changes fastest.
Arguments:
- hidden: bfloat16 [2048, 26624], P(('depth', 'row'), 'col'), may hold values from -6 to 6
- grad_out: bfloat16 [2048, 8192], P(('depth', 'col'), 'row'), may hold values from -6 to 6
- weight: bfloat16 [26624, 8192], P('col', 'row'), may hold values from -0.0390625 to 0.0390625
Outputs:
- hidden_gradient: bfloat16 [2048, 26624], P(('depth', 'row'), 'col')
- down_matrix_derivative: bfloat16 [26624, 8192], P('col', ('depth', 'row'))
All inputs are finite; a program needn't handle non-finite values.
Results may differ from a plain program's by a relative error of at most 0.005.
Values may be sent and summed in bfloat16 or wider, within the bound.
A program may use at most 128 MiB of HBM per device.

v0:
```python
import jax
import jax.numpy as jnp
from jax import lax
from jax.sharding import PartitionSpec as P


def shards(hidden, grad_out, weight):
    result_derivative_level = lax.all_gather(grad_out, "col", axis=0, tiled=True)
    slab_rows = result_derivative_level.shape[0]
    width_rows = result_derivative_level.shape[1]
    hidden_columns = weight.shape[0]
    replica_depth_count = lax.axis_size("depth")
    sub_width = width_rows // replica_depth_count
    derivative_multiplier = (slab_rows * replica_depth_count) ** (-0.5)
    local_lines = hidden.shape[0]
    whole_term = lax.dot_general(
        result_derivative_level,
        weight,
        (((1,), (1,)), ((), ())),
        preferred_element_type=jnp.float32,
    )
    total = lax.psum(whole_term, "row")
    start = lax.axis_index("row") * local_lines
    hidden_gradient = lax.dynamic_slice_in_dim(total, start, local_lines, 0).astype(jnp.bfloat16)
    pieces = result_derivative_level.reshape(slab_rows, replica_depth_count, sub_width)
    spread = lax.all_to_all(
        lax.all_to_all(pieces, "row", split_axis=1, concat_axis=1, tiled=True),
        "depth",
        split_axis=1,
        concat_axis=0,
        tiled=True,
    )
    result_derivative_pieces = spread.reshape(replica_depth_count, slab_rows, sub_width)
    h_all = lax.all_gather(hidden, ("depth", "row"), axis=0, tiled=True)
    activation_pieces_list = h_all.reshape(replica_depth_count, slab_rows, hidden_columns)
    token_slab_parts = jnp.einsum(
        "jcm,jco->jmo",
        activation_pieces_list,
        result_derivative_pieces,
        preferred_element_type=jnp.float32,
    )
    token_slab_parts = (token_slab_parts * derivative_multiplier).astype(jnp.bfloat16)
    token_slab_parts = lax.optimization_barrier(token_slab_parts)
    down_matrix_derivative = jnp.sum(token_slab_parts.astype(jnp.float32), axis=0).astype(
        jnp.bfloat16
    )
    return (hidden_gradient, down_matrix_derivative)


def solution(mesh):
    return jax.shard_map(
        shards,
        mesh=mesh,
        in_specs=(P(("depth", "row"), "col"), P(("depth", "col"), "row"), P("col", "row")),
        out_specs=(P(("depth", "row"), "col"), P("col", ("depth", "row"))),
        check_vma=False,
    )
```

profile of v0, /device:TPU:1, one launch (start us, length us, event | category | flops | bytes accessed | tf_op | source)
XLA Modules:
  0.0 314.1 jit_solution(9521337472969167857)
XLA Ops:
  7.2 0.0 all-gather.3.cloned.1.call-start
  7.2 0.7 all-gather.3.cloned.1.call-update
  7.9 0.0 all-gather.5.cloned.1.call-start
  7.9 0.7 all-gather.5.cloned.1.call-update
  8.7 58.6 %all-gather.3.cloned.1.call-done = bf16[512,2048]{1,0:T(8,128)(2,1)} async-done(((bf16[64,2048]{1,0:T(8,128)(2,1)}), bf16[512,2048]{1,0:T(8,128)(2,1)}) %all-gather.3.cloned.1.call-update) | async-done | bytes 2097168 | tf_op jit(solution)/shard_map/all_gather | solution.py:8
  67.3 2.9 copy.8
  70.1 2.4 copy.9
  72.5 4.4 %all-to-all-start = ((bf16[512,4,512]{2,0,1:T(8,128)(2,1)}), bf16[512,4,512]{2,0,1:T(8,128)(2,1)}, u32[]{:S(2)}, u32[]{:S(2)}) async-start(bf16[512,4,512]{2,0,1:T(8,128)(2,1)} %copy.9), calls=%async_computation | async-start | bytes 4194304 | tf_op jit(solution)/shard_map/all_to_all | solution.py:27
  77.0 13.6 %fusion.1 = f32[512,3328]{1,0:T(8,128)} fusion(bf16[512,2048]{1,0:T(8,128)(2,1)} %all-gather.3.cloned.1.call-done, bf16[3328,2048]{1,0:T(8,128)(2,1)} %param.5), kind=kOutput, calls=%fused_computation.3 | convolution fusion | flops 6979321856 | bytes 22544384 | tf_op jit(solution)/shard_map/dot_general | solution.py:16
  90.6 22.9 %all-to-all-done = bf16[512,4,512]{2,0,1:T(8,128)(2,1)} async-done(((bf16[512,4,512]{2,0,1:T(8,128)(2,1)}), bf16[512,4,512]{2,0,1:T(8,128)(2,1)}, u32[]{:S(2)}, u32[]{:S(2)}) %all-to-all-start) | async-done | bytes 2097184 | tf_op jit(solution)/shard_map/all_to_all | solution.py:27
  113.4 7.6 %all-to-all-start.1 = ((bf16[512,4,512]{2,0,1:T(8,128)(2,1)}), bf16[512,4,512]{2,0,1:T(8,128)(2,1)}, u32[]{:S(2)}, u32[]{:S(2)}) async-start(bf16[512,4,512]{2,0,1:T(8,128)(2,1)} %all-to-all-done), calls=%async_computation.1 | async-start | bytes 4194304 | tf_op jit(solution)/shard_map/all_to_all | solution.py:26
  121.0 161.5 %all-reduce.1 = bf16[512,3328]{1,0:T(8,128)(2,1)S(1)} all-reduce(f32[512,3328]{1,0:T(8,128)} %fusion.1), channel_id=1, replica_groups=mesh['depth'=4,'row'=4,'col'=8] {'row'}, use_global_device_ids=true, to_apply=%region_0.0 | all-reduce | flops 1703936 | bytes 10223616 | tf_op jit(solution)/shard_map/psum | solution.py:22
  282.6 1.0 dynamic-slice_convert_fusion
  283.5 0.0 all-to-all-done.1
  283.5 0.0 all-gather.5.cloned.1.call-done
  283.5 14.0 %multiply_convert_fusion = bf16[4,3328,512]{2,1,0:T(8,128)(2,1)} fusion(bf16[4,512,3328]{2,1,0:T(8,128)(2,1)} %bitcast.13, bf16[512,4,512]{2,0,1:T(8,128)(2,1)} %all-to-all-done.1), kind=kOutput, calls=%fused_computation | convolution fusion | flops 6992953344 | bytes 29360128 | tf_op jit(solution)/shard_map/jcm,jco->jmo/dot_general | solution.py:36
  297.5 9.8 %reduce_sum.12 = bf16[3328,512]{1,0:T(8,128)(2,1)} reduce(bf16[4,3328,512]{2,1,0:T(8,128)(2,1)} %multiply_convert_fusion, bf16[]{:T(256)} %constant.15.clone.1), dimensions={0}, to_apply=%region_1.0 | reduce | flops 5111808 | bytes 17039362 | tf_op jit(solution)/shard_map/reduce_sum | solution.py:44
Async XLA Ops:
  7.2 60.1 %all-gather.3.cloned.1.call-start = ((), (), s32[]{:S(2)}) async-start(), calls=%async_computation.2 | async-start | bytes 2359296 | tf_op jit(solution)/shard_map/all_gather | solution.py:8
  7.9 275.6 %all-gather.5.cloned.1.call-start = ((), (), s32[]{:S(2)}) async-start(), calls=%async_computation.3 | async-start | bytes 14483456 | tf_op jit(solution)/shard_map/all_gather | solution.py:34
  72.5 40.9 %all-to-all-start = ((bf16[512,4,512]{2,0,1:T(8,128)(2,1)}), bf16[512,4,512]{2,0,1:T(8,128)(2,1)}, u32[]{:S(2)}, u32[]{:S(2)}) async-start(bf16[512,4,512]{2,0,1:T(8,128)(2,1)} %copy.9), calls=%async_computation | async-start | bytes 4194304 | tf_op jit(solution)/shard_map/all_to_all | solution.py:27
  113.4 170.1 %all-to-all-start.1 = ((bf16[512,4,512]{2,0,1:T(8,128)(2,1)}), bf16[512,4,512]{2,0,1:T(8,128)(2,1)}, u32[]{:S(2)}, u32[]{:S(2)}) async-start(bf16[512,4,512]{2,0,1:T(8,128)(2,1)} %all-to-all-done), calls=%async_computation.1 | async-start | bytes 4194304 | tf_op jit(solution)/shard_map/all_to_all | solution.py:26
Sparse Core Ops, SparseCore 0:
  10.3 56.9 all-gather.2
  68.9 184.4 all-gather.4
where the time goes:
time: 315 us; the launch traced here: 314 us
  blocking collectives  162 us (51%)
  waiting for transfers between devices  82.9 us (26%)
  matrix products  27.6 us (9%)
  between operations  14.1 us (4%)
  starting transfers between devices  12.1 us (4%)
  other arithmetic  9.77 us (3%)
  local copies, waits for them, and re-layouts  6.19 us (2%)
    psum x1, blocking collectives, shards(): total = lax.psum(whole_term, 'row')  162 us
    all_gather x1, waiting for transfers between devices, shards(): lax.all_gather(grad_out, 'col', axis=0, tiled=True)  58.6 us
    all_to_all x1, waiting for transfers between devices, shards(): lax.all_to_all(pieces, 'row', split_axis=1, concat_axis=1, tiled=True)  22.9 us
    dot_general x1, matrix products, shards(): jnp.einsum('jcm,jco->jmo', activation_pieces_list, result_derivative_piec...  14 us
    dot_general x1, matrix products, shards(): lax.dot_general(result_derivative_level, weight, (((1,), (1,)), ((), ()))...  13.6 us
    reduce_sum x1, other arithmetic, shards(): jnp.sum(token_slab_parts.astype(jnp.float32), axis=0).astype(jnp.bfloat16)  9.77 us
    all_to_all x1, starting transfers between devices, shards(): lax.all_to_all(lax.all_to_all(pieces, 'row', split_axis=1, concat_axis=1,...  7.56 us
  transfers between devices with their start and end apart: 4, of which 2 were waited for; matrix products, arithmetic and copies ran while one was open for 6% of the time, Pallas kernels for 0%

commit v1 on v0

v1 whole, which is shorter than its diff:
```python
import jax
import jax.numpy as jnp
from jax import lax
from jax.experimental import pallas as pl
from jax.experimental.pallas import tpu as pltpu
from jax.sharding import PartitionSpec as P

MESH = pl.DeviceIdType.MESH
BF16 = jnp.bfloat16
F32 = jnp.float32

T, F, U, M = 128, 3328, 64, 2048
SUB = M // 4
HALF = T // 2
TILE = 256
B_LO, B_HI = 16, 32
B0, B1 = HALF - B_LO, HALF + B_HI
LO, HI = (0, HALF), (HALF, T)
ALO, B, AHI = (0, B0), (B0, B1), (B1, T)
BLO, BHI = (B0, HALF), (HALF, B1)
SCALE = 2048.0 ** -0.5


def slot(dz, dk, dx):
    return dk * 4 + dx if dz == 0 else 8 + ((dx + 1) % 4) * 2 + dk


def kernel(
    h_ref, g_ref, w_ref, hg_ref, dw_ref,
    hb, wv, g1, st, g2, own, pb, r1, r2, acc, dwv, hgv,
    ssem, rsem, a2s, a2r, lsem, osem,
):
    d, r, c = lax.axis_index("depth"), lax.axis_index("row"), lax.axis_index("col")
    zl, k, zh, y = d // 2, d % 2, c // 4, c % 4
    xp, xm = (d, (r + 1) % 4, c), (d, (r + 3) % 4, c)
    zp, sib = ((1 - zl) * 2 + k, r, c), (zl * 2 + 1 - k, r, c)
    ys = [(d, r, zh * 4 + (y + i) % 4) for i in (1, 2, 3)]
    zhp = (d, r, (1 - zh) * 4 + y)

    def place(col, row):
        return ((col // 2 + 4 - row) % 4) * 2 + col % 2

    mine, other = place(c, r), place((1 - zh) * 4 + y, r)
    same = d == r

    local = [
        pltpu.make_async_copy(w_ref, wv, lsem.at[0]),
        pltpu.make_async_copy(h_ref, hb.at[slot(0, 0, 0)], lsem.at[1]),
        pltpu.make_async_copy(g_ref, g1.at[mine], lsem.at[2]),
    ]
    for cp in reversed(local):
        cp.start()

    barrier = pltpu.get_barrier_semaphore()
    for who in [xp, xm, zp, sib, zhp] + ys:
        pl.semaphore_signal(barrier, inc=1, device_id=who, device_id_type=MESH)
    for i in range(4):
        source = ((d + i) % 4, d, c)
        if i == 0:
            @pl.when(jnp.logical_not(same))
            def _():
                pl.semaphore_signal(barrier, inc=1, device_id=source, device_id_type=MESH)
        else:
            pl.semaphore_signal(barrier, inc=1, device_id=source, device_id_type=MESH)
    pl.semaphore_wait(barrier, 12 - same.astype(jnp.int32))

    copies = {}

    def send(key, src, dst, to):
        n = len(copies)
        cp = pltpu.make_async_remote_copy(
            src_ref=src, dst_ref=dst, send_sem=ssem.at[n], recv_sem=rsem.at[n],
            device_id=to, device_id_type=MESH,
        )
        cp.start()
        copies[key] = cp

    def got(*keys):
        for key in keys:
            copies[key].wait_recv()

    def rows(s, span):
        return hb.at[s, pl.ds(span[0], span[1] - span[0])]

    def pass_on(name, to, src, dst, span):
        send((name, dst, span), rows(src, span), rows(dst, span), to)

    rel = ((zl + r // 2) % 2) * 2 + (k + r % 2) % 2
    a2a = []
    for i in range(4):
        j = (r + i) % 4
        src = g_ref.at[:, pl.ds(pl.multiple_of(j * SUB, SUB), SUB)]
        dst = st.at[place(c, j), rel]
        cp = pltpu.make_async_remote_copy(
            src_ref=src, dst_ref=dst, send_sem=a2s.at[i], recv_sem=a2r.at[rel],
            device_id=(r, j, c), device_id_type=MESH,
        )
        a2a.append(cp)
        if i == 0:
            @pl.when(jnp.logical_not(same))
            def _():
                cp.start()

            @pl.when(same)
            def _():
                pltpu.make_async_copy(src, dst, a2r.at[0]).start()
        else:
            cp.start()

    send("g1z", g_ref, g1.at[mine], zhp)
    for i in range(3):
        send(("g1y", i), g_ref, g1.at[mine], ys[i])

    def h_own(name, to, dst, span):
        send((name, dst, span), h_ref.at[pl.ds(span[0], span[1] - span[0])], rows(dst, span), to)

    h_own("z", zp, slot(1, 0, 0), B)
    h_own("x", xp, slot(0, 0, 3), LO)
    h_own("x", xm, slot(0, 0, 1), HI)
    h_own("x", xp, slot(0, 0, 3), HI)
    h_own("x", xm, slot(0, 0, 1), LO)
    h_own("z", zp, slot(1, 0, 0), ALO)
    h_own("z", zp, slot(1, 0, 0), AHI)
    h_own("s", sib, slot(0, 1, 0), (0, T))

    got("g1z")
    for i in range(3):
        send(("g1zy", i), g1.at[other], g1.at[other], ys[i])

    for i in range(4):
        pltpu.make_async_copy(st.at[0, i], st.at[0, i], a2r.at[i]).wait()
    send("g2z", st.at[mine], st.at[mine], zhp)
    for i in range(3):
        send(("g2y", i), st.at[mine], st.at[mine], ys[i])

    def near(dx, half, part, to):
        s = slot(0, 0, dx)
        got(("x", s, half))
        if to is not None:
            pass_on("x", to, s, slot(0, 0, 2), half)
        pass_on("z", zp, s, slot(1, 0, dx), part)
        pass_on("s", sib, s, slot(0, 1, dx), half)

    near(3, LO, ALO, xp)
    near(1, HI, AHI, xm)

    got("g2z")
    for i in range(3):
        send(("g2zy", i), st.at[other], st.at[other], ys[i])

    got(("z", slot(1, 0, 0), B))
    pass_on("x", xp, slot(1, 0, 0), slot(1, 0, 3), B)
    pass_on("x", xm, slot(1, 0, 0), slot(1, 0, 1), B)

    near(3, HI, AHI, None)
    near(1, LO, ALO, None)

    local[0].wait()
    local[2].wait()
    got(*[("g1y", i) for i in range(3)], *[("g1zy", i) for i in range(3)])

    @pl.loop(0, F // TILE)
    def _(n):
        at = pl.ds(pl.multiple_of(n * TILE, TILE), TILE)
        p = lax.dot_general(
            g1[...].reshape(8 * U, M), wv[at, :], (((1,), (1,)), ((), ())),
            preferred_element_type=F32,
        )
        own[:, at] = p[:T]
        for j in range(3):
            pb[j, :, at] = p[T * (j + 1) : T * (j + 2)].astype(BF16)

    lo, hi = pl.ds(0, HALF), pl.ds(HALF, HALF)
    send("r1lo", pb.at[1, lo], r1.at[0], xm)
    send("r1hi", pb.at[1, hi], r1.at[1], xp)
    send("r2alo", pb.at[0, lo], r2.at[0, lo], xp)
    send("r2bhi", pb.at[2, hi], r2.at[1, hi], xm)

    s = slot(0, 0, 2)
    for half, part in ((LO, ALO), (HI, AHI)):
        got(("x", s, half))
        pass_on("z", zp, s, slot(1, 0, 2), part)
        pass_on("s", sib, s, slot(0, 1, 2), half)

    got(("z", slot(1, 0, 0), ALO), ("z", slot(1, 0, 0), AHI))
    pass_on("s", sib, slot(1, 0, 0), slot(1, 1, 0), (0, T))

    got(("x", slot(1, 0, 3), B))
    pass_on("x", xp, slot(1, 0, 3), slot(1, 0, 2), BLO)
    got(("x", slot(1, 0, 1), B))
    pass_on("x", xm, slot(1, 0, 1), slot(1, 0, 2), BHI)

    got("r1lo")
    pb[2, lo, :] = (pb[2, lo, :].astype(F32) + r1[0].astype(F32)).astype(BF16)
    send("r2blo", pb.at[2, lo], r2.at[1, lo], xm)
    got("r1hi")
    pb[0, hi, :] = (pb[0, hi, :].astype(F32) + r1[1].astype(F32)).astype(BF16)
    send("r2ahi", pb.at[0, hi], r2.at[0, hi], xp)

    got(*[("g2y", i) for i in range(3)], *[("g2zy", i) for i in range(3)])
    for dz in range(2):
        for dk in range(2):
            for dx in range(4):
                for half in range(2):
                    g2[slot(dz, dk, dx), half * U : (half + 1) * U, :] = st[dx * 2 + half, dz * 2 + dk]

    def product(first, last, at):
        depth = (last - first) * T
        return lax.dot_general(
            hb[first:last, :, at].reshape(depth, TILE), g2[first:last].reshape(depth, SUB),
            (((0,), (0,)), ((), ())), preferred_element_type=F32,
        )

    local[1].wait()
    got(("s", slot(0, 1, 0), (0, T)))
    for dx in (1, 2, 3):
        got(("s", slot(0, 1, dx), LO), ("s", slot(0, 1, dx), HI))

    @pl.loop(0, F // TILE)
    def _(n):
        at = pl.ds(pl.multiple_of(n * TILE, TILE), TILE)
        acc[at, :] = product(0, 8, at)

    for dx in (3, 1):
        got(("z", slot(1, 0, dx), ALO), ("z", slot(1, 0, dx), AHI))
        pass_on("s", sib, slot(1, 0, dx), slot(1, 1, dx), (0, T))

    got("r2alo", "r2bhi", "r2blo", "r2ahi")
    hgv[...] = (own[...] + r2[0].astype(F32) + r2[1].astype(F32)).astype(BF16)
    hg_copy = pltpu.make_async_copy(hgv, hg_ref, lsem.at[3])
    hg_copy.start()

    for dx in (0, 1, 3):
        got(("s", slot(1, 1, dx), (0, T)))

    @pl.loop(0, F // TILE)
    def _(n):
        at = pl.ds(pl.multiple_of(n * TILE, TILE), TILE)
        acc[at, :] += product(8, 14, at)

    s = slot(1, 0, 2)
    for name, part in (("x", BLO), ("x", BHI), ("z", ALO), ("z", AHI)):
        got((name, s, part))
        pass_on("s", sib, s, slot(1, 1, 2), part)
    for part in (BLO, BHI, ALO, AHI):
        got(("s", slot(1, 1, 2), part))

    @pl.loop(0, F // TILE)
    def _(n):
        at = pl.ds(pl.multiple_of(n * TILE, TILE), TILE)
        dwv[at, :] = ((acc[at, :] + product(14, 16, at)) * SCALE).astype(BF16)
        pltpu.make_async_copy(dwv.at[at], dw_ref.at[at], osem.at[n]).start()

    @pl.loop(0, F // TILE)
    def _(n):
        at = pl.ds(pl.multiple_of(n * TILE, TILE), TILE)
        pltpu.make_async_copy(dwv.at[at], dw_ref.at[at], osem.at[n]).wait()

    hg_copy.wait()
    for cp in copies.values():
        cp.wait_send()
    for i in range(1, 4):
        a2a[i].wait_send()

    @pl.when(jnp.logical_not(same))
    def _():
        a2a[0].wait_send()


def shards(hidden, grad_out, weight):
    return pl.pallas_call(
        kernel,
        out_shape=(jax.ShapeDtypeStruct((T, F), BF16), jax.ShapeDtypeStruct((F, SUB), BF16)),
        in_specs=[pl.BlockSpec(memory_space=pl.ANY)] * 3,
        out_specs=(pl.BlockSpec(memory_space=pl.ANY), pl.BlockSpec(memory_space=pl.ANY)),
        scratch_shapes=[
            pltpu.VMEM((16, T, F), BF16),
            pltpu.VMEM((F, M), BF16),
            pltpu.VMEM((8, U, M), BF16),
            pltpu.VMEM((8, 4, U, SUB), BF16),
            pltpu.VMEM((16, T, SUB), BF16),
            pltpu.VMEM((T, F), F32),
            pltpu.VMEM((3, T, F), BF16),
            pltpu.VMEM((2, HALF, F), BF16),
            pltpu.VMEM((2, T, F), BF16),
            pltpu.VMEM((F, SUB), F32),
            pltpu.VMEM((F, SUB), BF16),
            pltpu.VMEM((T, F), BF16),
            pltpu.SemaphoreType.DMA((64,)),
            pltpu.SemaphoreType.DMA((64,)),
            pltpu.SemaphoreType.DMA((4,)),
            pltpu.SemaphoreType.DMA((4,)),
            pltpu.SemaphoreType.DMA((4,)),
            pltpu.SemaphoreType.DMA((F // TILE,)),
        ],
        compiler_params=pltpu.CompilerParams(
            collective_id=0, has_side_effects=True, vmem_limit_bytes=60 * 2**20
        ),
        cost_estimate=pl.CostEstimate(
            flops=4 * 512 * M * F, bytes_accessed=2 * F * (M + SUB + 2 * T), transcendentals=0
        ),
    )(hidden, grad_out, weight)


def solution(mesh):
    return jax.shard_map(
        shards,
        mesh=mesh,
        in_specs=(P(("depth", "row"), "col"), P(("depth", "col"), "row"), P("col", "row")),
        out_specs=(P(("depth", "row"), "col"), P("col", ("depth", "row"))),
        check_vma=False,
    )
```

time: 315 us -> 105 us (0.33)
  blocking collectives: 162 us -> 0 us
  Pallas kernels: 0 us -> 97.7 us
  waiting for transfers between devices: 82.9 us -> 0 us
  matrix products: 27.6 us -> 0 us
  between operations: 14.1 us -> 0.64 us
  starting transfers between devices: 12.1 us -> 0 us
  other arithmetic: 9.77 us -> 0 us
    psum x1 -> x0, blocking collectives: 162 us -> none  [shards(): total = lax.psum(whole_term, 'row')]
    pallas_call x0 -> x1, Pallas kernels: none -> 97.7 us  [shards(): pl.pallas_call(kernel, out_shape=(jax.ShapeDtypeStruct((T, F), BF16), jax...]
    all_gather x2 -> x0, waiting for transfers between devices: 58.6 us -> none  [the longest x1 58.6 us: shards(): lax.all_gather(grad_out, 'col', axis=0, tiled=True)]
    dot_general x2 -> x0, matrix products: 27.6 us -> none  [the longest x1 14 us: shards(): jnp.einsum('jcm,jco->jmo', activation_pieces_list, result_derivative_piec...]
    all_to_all x2 -> x0, waiting for transfers between devices: 22.9 us -> none  [the longest x1 22.9 us: shards(): lax.all_to_all(pieces, 'row', split_axis=1, concat_axis=1, tiled=True)]
    all_to_all x2 -> x0, starting transfers between devices: 12 us -> none  [the longest x1 7.56 us: shards(): lax.all_to_all(lax.all_to_all(pieces, 'row', split_axis=1, concat_axis=1,...]
    reduce_sum x1 -> x0, other arithmetic: 9.77 us -> none  [shards(): jnp.sum(token_slab_parts.astype(jnp.float32), axis=0).astype(jnp.bfloat16)]
    unnamed x0 -> x2, local copies, waits for them, and re-layouts: none -> 6.04 us
  transfers between devices with their start and end apart: 4 -> 0, of which waited for: 2 -> 0; matrix products, arithmetic and copies ran while one was open for 6% -> 0% of each run, Pallas kernels for 0% -> 0%
where the time goes in v1:
time: 105 us; the launch traced here: 104 us
  Pallas kernels  97.7 us (93%)
  local copies, waits for them, and re-layouts  6.04 us (6%)
    pallas_call x1, Pallas kernels, shards(): pl.pallas_call(kernel, out_shape=(jax.ShapeDtypeStruct((T, F), BF16), jax...  97.7 us
    unnamed x2, local copies, waits for them, and re-layouts  6.04 us

profile of v1, /device:TPU:1, one launch (start us, length us, event | category | flops | bytes accessed | tf_op | source)
XLA Modules:
  0.0 104.4 jit_solution(2723405448278333520)
XLA Ops:
  0.6 97.7 %shard_map.50 = (bf16[128,3328]{1,0:T(8,128)(2,1)}, bf16[3328,512]{1,0:T(8,128)(2,1)}) custom-call(bf16[128,3328]{1,0:T(8,128)(2,1)} %h_ref.1, bf16[64,2048]{1,0:T(8,128)(2,1)} %g_ref.1, bf16[3328,2048]{1,0:T(8,128)(2,1)} %w_ref.1), custom_call_target="tpu_custom_call" | custom-call | flops 13958643712 | bytes 18743296 | tf_op jit(solution)/shard_map/pallas_call | solution.py:271
  98.3 2.1 %copy.7 = bf16[128,3328]{1,0:T(8,128)(2,1)} copy(bf16[128,3328]{1,0:T(8,128)(2,1)} %get-tuple-element.4) | data formatting | bytes 1703936
  100.4 3.9 %copy.8 = bf16[3328,512]{1,0:T(8,128)(2,1)} copy(bf16[3328,512]{1,0:T(8,128)(2,1)} %get-tuple-element.5) | data formatting | bytes 6815744

commit v2 on v1

--- a/solution.py
+++ b/solution.py
@@ -119,8 +119,6 @@
     h_own("x", xm, slot(0, 0, 1), HI)
     h_own("x", xp, slot(0, 0, 3), HI)
     h_own("x", xm, slot(0, 0, 1), LO)
-    h_own("z", zp, slot(1, 0, 0), ALO)
-    h_own("z", zp, slot(1, 0, 0), AHI)
     h_own("s", sib, slot(0, 1, 0), (0, T))
 
     got("g1z")
@@ -132,6 +130,8 @@
     send("g2z", st.at[mine], st.at[mine], zhp)
     for i in range(3):
         send(("g2y", i), st.at[mine], st.at[mine], ys[i])
+    h_own("z", zp, slot(1, 0, 0), ALO)
+    h_own("z", zp, slot(1, 0, 0), AHI)
 
     def near(dx, half, part, to):
         s = slot(0, 0, dx)
@@ -144,10 +144,6 @@
     near(3, LO, ALO, xp)
     near(1, HI, AHI, xm)
 
-    got("g2z")
-    for i in range(3):
-        send(("g2zy", i), st.at[other], st.at[other], ys[i])
-
     got(("z", slot(1, 0, 0), B))
     pass_on("x", xp, slot(1, 0, 0), slot(1, 0, 3), B)
     pass_on("x", xm, slot(1, 0, 0), slot(1, 0, 1), B)
@@ -176,6 +172,10 @@
     send("r2alo", pb.at[0, lo], r2.at[0, lo], xp)
     send("r2bhi", pb.at[2, hi], r2.at[1, hi], xm)
 
+    got("g2z")
+    for i in range(3):
+        send(("g2zy", i), st.at[other], st.at[other], ys[i])
+
     s = slot(0, 0, 2)
     for half, part in ((LO, ALO), (HI, AHI)):
         got(("x", s, half))
@@ -189,6 +189,30 @@
     pass_on("x", xp, slot(1, 0, 3), slot(1, 0, 2), BLO)
     got(("x", slot(1, 0, 1), B))
     pass_on("x", xm, slot(1, 0, 1), slot(1, 0, 2), BHI)
+
+    got(*[("g2y", i) for i in range(3)], *[("g2zy", i) for i in range(3)])
+    for dz in range(2):
+        for dk in range(2):
+            for dx in range(4):
+                for half in range(2):
+                    g2[slot(dz, dk, dx), half * U : (half + 1) * U, :] = st[dx * 2 + half, dz * 2 + dk]
+
+    def product(first, last, at):
+        depth = (last - first) * T
+        return lax.dot_general(
+            hb[first:last, :, at].reshape(depth, TILE), g2[first:last].reshape(depth, SUB),
+            (((0,), (0,)), ((), ())), preferred_element_type=F32,
+        )
+
+    local[1].wait()
+    got(("s", slot(0, 1, 0), (0, T)))
+    for dx in (1, 2, 3):
+        got(("s", slot(0, 1, dx), LO), ("s", slot(0, 1, dx), HI))
+
+    @pl.loop(0, F // TILE)
+    def _(n):
+        at = pl.ds(pl.multiple_of(n * TILE, TILE), TILE)
+        acc[at, :] = product(0, 8, at)
 
     got("r1lo")
     pb[2, lo, :] = (pb[2, lo, :].astype(F32) + r1[0].astype(F32)).astype(BF16)
@@ -197,38 +221,9 @@
     pb[0, hi, :] = (pb[0, hi, :].astype(F32) + r1[1].astype(F32)).astype(BF16)
     send("r2ahi", pb.at[0, hi], r2.at[0, hi], xp)
 
-    got(*[("g2y", i) for i in range(3)], *[("g2zy", i) for i in range(3)])
-    for dz in range(2):
-        for dk in range(2):
-            for dx in range(4):
-                for half in range(2):
-                    g2[slot(dz, dk, dx), half * U : (half + 1) * U, :] = st[dx * 2 + half, dz * 2 + dk]
-
-    def product(first, last, at):
-        depth = (last - first) * T
-        return lax.dot_general(
-            hb[first:last, :, at].reshape(depth, TILE), g2[first:last].reshape(depth, SUB),
-            (((0,), (0,)), ((), ())), preferred_element_type=F32,
-        )
-
-    local[1].wait()
-    got(("s", slot(0, 1, 0), (0, T)))
-    for dx in (1, 2, 3):
-        got(("s", slot(0, 1, dx), LO), ("s", slot(0, 1, dx), HI))
-
-    @pl.loop(0, F // TILE)
-    def _(n):
-        at = pl.ds(pl.multiple_of(n * TILE, TILE), TILE)
-        acc[at, :] = product(0, 8, at)
-
     for dx in (3, 1):
         got(("z", slot(1, 0, dx), ALO), ("z", slot(1, 0, dx), AHI))
         pass_on("s", sib, slot(1, 0, dx), slot(1, 1, dx), (0, T))
-
-    got("r2alo", "r2bhi", "r2blo", "r2ahi")
-    hgv[...] = (own[...] + r2[0].astype(F32) + r2[1].astype(F32)).astype(BF16)
-    hg_copy = pltpu.make_async_copy(hgv, hg_ref, lsem.at[3])
-    hg_copy.start()
 
     for dx in (0, 1, 3):
         got(("s", slot(1, 1, dx), (0, T)))
@@ -250,6 +245,11 @@
         at = pl.ds(pl.multiple_of(n * TILE, TILE), TILE)
         dwv[at, :] = ((acc[at, :] + product(14, 16, at)) * SCALE).astype(BF16)
         pltpu.make_async_copy(dwv.at[at], dw_ref.at[at], osem.at[n]).start()
+
+    got("r2alo", "r2bhi", "r2blo", "r2ahi")
+    hgv[...] = (own[...] + r2[0].astype(F32) + r2[1].astype(F32)).astype(BF16)
+    hg_copy = pltpu.make_async_copy(hgv, hg_ref, lsem.at[3])
+    hg_copy.start()
 
     @pl.loop(0, F // TILE)
     def _(n):

time: 105 us -> 87.7 us (0.84)
  Pallas kernels: 97.7 us -> 80.9 us
    pallas_call x1, Pallas kernels: 97.7 us -> 80.9 us  [shards(): pl.pallas_call(kernel, out_shape=(jax.ShapeDtypeStruct((T, F), BF16), jax...]
where the time goes in v2:
time: 87.7 us; the launch traced here: 87.6 us
  Pallas kernels  80.9 us (92%)
  local copies, waits for them, and re-layouts  6.04 us (7%)
    pallas_call x1, Pallas kernels, shards(): pl.pallas_call(kernel, out_shape=(jax.ShapeDtypeStruct((T, F), BF16), jax...  80.9 us
    unnamed x2, local copies, waits for them, and re-layouts  6.04 us

profile of v2, /device:TPU:1, one launch (start us, length us, event | category | flops | bytes accessed | tf_op | source)
XLA Modules:
  0.0 87.6 jit_solution(5366077007190388803)
XLA Ops:
  0.6 80.9 %shard_map.50 = (bf16[128,3328]{1,0:T(8,128)(2,1)}, bf16[3328,512]{1,0:T(8,128)(2,1)}) custom-call(bf16[128,3328]{1,0:T(8,128)(2,1)} %h_ref.1, bf16[64,2048]{1,0:T(8,128)(2,1)} %g_ref.1, bf16[3328,2048]{1,0:T(8,128)(2,1)} %w_ref.1), custom_call_target="tpu_custom_call" | custom-call | flops 13958643712 | bytes 18743296 | tf_op jit(solution)/shard_map/pallas_call | solution.py:271
  81.5 2.1 %copy.7 = bf16[128,3328]{1,0:T(8,128)(2,1)} copy(bf16[128,3328]{1,0:T(8,128)(2,1)} %get-tuple-element.4) | data formatting | bytes 1703936
  83.6 3.9 %copy.8 = bf16[3328,512]{1,0:T(8,128)(2,1)} copy(bf16[3328,512]{1,0:T(8,128)(2,1)} %get-tuple-element.5) | data formatting | bytes 6815744

commit v3 on v2

v3 whole, which is shorter than its diff:
```python
import jax
import jax.numpy as jnp
from jax import lax
from jax.experimental import pallas as pl
from jax.experimental.pallas import tpu as pltpu
from jax.sharding import PartitionSpec as P

MESH = pl.DeviceIdType.MESH
BF16 = jnp.bfloat16
F32 = jnp.float32

T, F, U, M = 128, 3328, 64, 2048
SUB = M // 4
HALF = T // 2
TILE = 256
NW = 4
B_LO, B_HI = 16, 32
B0, B1 = HALF - B_LO, HALF + B_HI
LO, HI = (0, HALF), (HALF, T)
ALO, B, AHI = (0, B0), (B0, B1), (B1, T)
BLO, BHI = (B0, HALF), (HALF, B1)
COLS = ((0, 7 * TILE), (7 * TILE, F))
SCALE = 2048.0 ** -0.5


def slot(dz, dk, dx):
    return dk * 4 + dx if dz == 0 else 8 + (0, 1, 3, 2)[dx] * 2 + dk


def kernel(
    h_ref, g_ref, w_ref, hg_ref, dw_ref,
    hb, wv, g1, st, g2, own, pb, r1, r2, acc, dwv, hgv,
    ssem, rsem, a2s, a2r, lsem, osem, wsem,
):
    d, r, c = lax.axis_index("depth"), lax.axis_index("row"), lax.axis_index("col")
    zl, k, zh, y = d // 2, d % 2, c // 4, c % 4
    xp, xm = (d, (r + 1 + 2 * k) % 4, c), (d, (r + 3 - 2 * k) % 4, c)
    zp, sib = ((1 - zl) * 2 + k, r, c), (zl * 2 + 1 - k, r, c)
    yp, ym = (d, r, zh * 4 + (y + 1) % 4), (d, r, zh * 4 + (y + 3) % 4)
    zhp = (d, r, (1 - zh) * 4 + y)

    def place(col, row, core):
        return ((1 + 2 * core) * (col // 2 + 4 - row) % 4) * 2 + col % 2

    mine, other = place(c, r, k), place((1 - zh) * 4 + y, r, k)
    same = d == r

    local = [
        pltpu.make_async_copy(h_ref, hb.at[slot(0, 0, 0)], lsem.at[0]),
        pltpu.make_async_copy(g_ref, g1.at[mine], lsem.at[1]),
    ]
    for cp in reversed(local):
        cp.start()

    def weight_tile(n):
        at = pl.ds(pl.multiple_of(n * TILE, TILE), TILE)
        return pltpu.make_async_copy(w_ref.at[at], wv.at[n % NW], wsem.at[n % NW])

    for n in range(NW):
        weight_tile(n).start()

    barrier = pltpu.get_barrier_semaphore()
    for who in (xp, xm, zp, sib, zhp, yp, ym):
        pl.semaphore_signal(barrier, inc=1, device_id=who, device_id_type=MESH)
    for i in range(4):
        source = ((d + i) % 4, d, c)
        if i == 0:
            @pl.when(jnp.logical_not(same))
            def _():
                pl.semaphore_signal(barrier, inc=1, device_id=source, device_id_type=MESH)
        else:
            pl.semaphore_signal(barrier, inc=1, device_id=source, device_id_type=MESH)
    pl.semaphore_wait(barrier, 11 - same.astype(jnp.int32))

    copies = {}

    def send(key, src, dst, to):
        n = len(copies)
        cp = pltpu.make_async_remote_copy(
            src_ref=src, dst_ref=dst, send_sem=ssem.at[n], recv_sem=rsem.at[n],
            device_id=to, device_id_type=MESH,
        )
        cp.start()
        copies[key] = cp

    def got(*keys):
        for key in keys:
            if isinstance(key, tuple) and len(key) == 3:
                key = (*key, (0, F))
            copies[key].wait_recv()

    def rows(s, span, cols=(0, F)):
        return hb.at[s, pl.ds(span[0], span[1] - span[0]), pl.ds(cols[0], cols[1] - cols[0])]

    def pass_on(name, to, src, dst, span, cols=(0, F)):
        send((name, dst, span, cols), rows(src, span, cols), rows(dst, span, cols), to)

    rel = ((zl + r // 2) % 2) * 2 + (k + r % 2) % 2
    a2a = []
    for i in range(4):
        j = (r + i) % 4
        src = g_ref.at[:, pl.ds(pl.multiple_of(j * SUB, SUB), SUB)]
        dst = st.at[place(c, j, r % 2), rel]
        cp = pltpu.make_async_remote_copy(
            src_ref=src, dst_ref=dst, send_sem=a2s.at[i], recv_sem=a2r.at[rel],
            device_id=(r, j, c), device_id_type=MESH,
        )
        a2a.append(cp)
        if i == 0:
            @pl.when(jnp.logical_not(same))
            def _():
                cp.start()

            @pl.when(same)
            def _():
                pltpu.make_async_copy(src, dst, a2r.at[0]).start()
        else:
            cp.start()

    def ring(name, src, dst):
        send((name, "p"), src, dst, yp)
        send((name, "m"), src, dst, ym)

    def ring_on(name, buf, layer, n):
        for way, off, at, to in (("p", 3, 0, yp), ("m", 1, n, ym)):
            part = buf.at[place(layer * 4 + (y + off) % 4, r, k), pl.ds(at, n)]
            got((name, way))
            send((name, 2 * way), part, part, to)

    send("g1z", g_ref, g1.at[mine], zhp)
    ring("g1y", g_ref, g1.at[mine])

    def h_own(name, to, dst, span):
        send((name, dst, span, (0, F)), h_ref.at[pl.ds(span[0], span[1] - span[0])], rows(dst, span), to)

    h_own("z", zp, slot(1, 0, 0), B)
    h_own("x", xp, slot(0, 0, 3), LO)
    h_own("x", xm, slot(0, 0, 1), HI)
    h_own("x", xp, slot(0, 0, 3), HI)
    h_own("x", xm, slot(0, 0, 1), LO)
    h_own("s", sib, slot(0, 1, 0), (0, T))

    got("g1z")
    ring("g1zy", g1.at[other], g1.at[other])
    ring_on("g1y", g1, zh, U // 2)

    for i in range(4):
        pltpu.make_async_copy(st.at[0, i], st.at[0, i], a2r.at[i]).wait()
    send("g2z", st.at[mine], st.at[mine], zhp)
    h_own("z", zp, slot(1, 0, 0), ALO)
    h_own("z", zp, slot(1, 0, 0), AHI)

    def near(dx, half, part, to):
        s = slot(0, 0, dx)
        got(("x", s, half))
        if to is not None:
            pass_on("x", to, s, slot(0, 0, 2), half)
        pass_on("z", zp, s, slot(1, 0, dx), part)
        pass_on("s", sib, s, slot(0, 1, dx), half)

    near(3, LO, ALO, xp)
    near(1, HI, AHI, xm)

    ring_on("g1zy", g1, 1 - zh, U // 2)
    ring("g2y", st.at[mine], st.at[mine])

    got(("z", slot(1, 0, 0), B))
    pass_on("x", xp, slot(1, 0, 0), slot(1, 0, 3), B)
    pass_on("x", xm, slot(1, 0, 0), slot(1, 0, 1), B)

    near(3, HI, AHI, None)
    near(1, LO, ALO, None)

    local[1].wait()
    got(("g1y", "pp"), ("g1y", "mm"), ("g1zy", "pp"), ("g1zy", "mm"))

    def feature_sums(n):
        at = pl.ds(pl.multiple_of(n * TILE, TILE), TILE)
        weight_tile(n).wait()
        p = lax.dot_general(
            g1[...].reshape(8 * U, M), wv[n % NW], (((1,), (1,)), ((), ())),
            preferred_element_type=F32,
        )
        own[:, at] = p[:T]
        for j in range(3):
            pb[j, :, at] = p[T * (j + 1) : T * (j + 2)].astype(BF16)

        @pl.when(n + NW < F // TILE)
        def _():
            weight_tile(n + NW).start()

    pl.loop(0, 7)(feature_sums)
    got("g2z")
    ring("g2zy", st.at[other], st.at[other])

    pl.loop(7, F // TILE)(feature_sums)

    lo, hi = pl.ds(0, HALF), pl.ds(HALF, HALF)
    send("r1lo", pb.at[1, lo], r1.at[0], xm)
    send("r1hi", pb.at[1, hi], r1.at[1], xp)
    send("r2alo", pb.at[0, lo], r2.at[0, lo], xp)
    send("r2bhi", pb.at[2, hi], r2.at[1, hi], xm)

    ring_on("g2y", st, zh, 2)
    ring_on("g2zy", st, 1 - zh, 2)

    s = slot(0, 0, 2)
    for half in (LO, HI):
        got(("x", s, half))
        pass_on("s", sib, s, slot(0, 1, 2), half)
    for cols in COLS:
        for part in (ALO, AHI):
            pass_on("z", zp, s, slot(1, 0, 2), part, cols)

    got(("z", slot(1, 0, 0), ALO), ("z", slot(1, 0, 0), AHI))
    pass_on("s", sib, slot(1, 0, 0), slot(1, 1, 0), (0, T))

    got(("x", slot(1, 0, 3), B))
    pass_on("x", xp, slot(1, 0, 3), slot(1, 0, 2), BLO)
    got(("x", slot(1, 0, 1), B))
    pass_on("x", xm, slot(1, 0, 1), slot(1, 0, 2), BHI)

    got(("g2y", "pp"), ("g2y", "mm"), ("g2zy", "pp"), ("g2zy", "mm"))
    for dz in range(2):
        for dk in range(2):
            for dx in range(4):
                for half in range(2):
                    g2[slot(dz, dk, dx), half * U : (half + 1) * U, :] = st[(-dx if dk else dx) % 4 * 2 + half, dz * 2 + dk]

    def product(first, last, at):
        depth = (last - first) * T
        return lax.dot_general(
            hb[first:last, :, at].reshape(depth, TILE), g2[first:last].reshape(depth, SUB),
            (((0,), (0,)), ((), ())), preferred_element_type=F32,
        )

    local[0].wait()
    got(("s", slot(0, 1, 0), (0, T)))
    for dx in (1, 2, 3):
        got(("s", slot(0, 1, dx), LO), ("s", slot(0, 1, dx), HI))
    got(("s", slot(1, 1, 0), (0, T)))

    @pl.loop(0, F // TILE)
    def _(n):
        at = pl.ds(pl.multiple_of(n * TILE, TILE), TILE)
        acc[at, :] = product(0, 10, at)

    got("r1lo")
    pb[2, lo, :] = (pb[2, lo, :].astype(F32) + r1[0].astype(F32)).astype(BF16)
    send("r2blo", pb.at[2, lo], r2.at[1, lo], xm)
    got("r1hi")
    pb[0, hi, :] = (pb[0, hi, :].astype(F32) + r1[1].astype(F32)).astype(BF16)
    send("r2ahi", pb.at[0, hi], r2.at[0, hi], xp)

    for dx in (3, 1):
        got(("z", slot(1, 0, dx), ALO), ("z", slot(1, 0, dx), AHI))
        pass_on("s", sib, slot(1, 0, dx), slot(1, 1, dx), (0, T))

    for dx in (1, 3):
        got(("s", slot(1, 1, dx), (0, T)))

    @pl.loop(0, F // TILE)
    def _(n):
        at = pl.ds(pl.multiple_of(n * TILE, TILE), TILE)
        acc[at, :] += product(10, 14, at)

    s = slot(1, 0, 2)
    for part in (BLO, BHI):
        got(("x", s, part))
        pass_on("s", sib, s, slot(1, 1, 2), part)
    for cols in COLS:
        for part in (ALO, AHI):
            got(("z", s, part, cols))
            pass_on("s", sib, s, slot(1, 1, 2), part, cols)
        if cols == COLS[0]:
            got(("s", slot(1, 1, 2), BLO), ("s", slot(1, 1, 2), BHI))
        for part in (ALO, AHI):
            got(("s", slot(1, 1, 2), part, cols))

        @pl.loop(cols[0] // TILE, cols[1] // TILE)
        def _(n):
            at = pl.ds(pl.multiple_of(n * TILE, TILE), TILE)
            dwv[at, :] = ((acc[at, :] + product(14, 16, at)) * SCALE).astype(BF16)
            pltpu.make_async_copy(dwv.at[at], dw_ref.at[at], osem.at[n]).start()

    got("r2alo", "r2bhi")
    own[lo, :] += r2[0, lo, :].astype(F32)
    own[hi, :] += r2[1, hi, :].astype(F32)
    hg_copies = []
    for i, (name, half) in enumerate((("r2blo", lo), ("r2ahi", hi))):
        got(name)
        hgv[half, :] = (own[half, :] + r2[1 - i, half, :].astype(F32)).astype(BF16)
        hg_copies.append(pltpu.make_async_copy(hgv.at[half], hg_ref.at[half], lsem.at[2 + i]))
        hg_copies[i].start()

    @pl.loop(0, F // TILE)
    def _(n):
        at = pl.ds(pl.multiple_of(n * TILE, TILE), TILE)
        pltpu.make_async_copy(dwv.at[at], dw_ref.at[at], osem.at[n]).wait()

    for cp in hg_copies:
        cp.wait()
    for cp in copies.values():
        cp.wait_send()
    for i in range(1, 4):
        a2a[i].wait_send()

    @pl.when(jnp.logical_not(same))
    def _():
        a2a[0].wait_send()


def shards(hidden, grad_out, weight):
    hidden, grad_out, weight = (pltpu.with_memory_space_constraint(a, pltpu.HBM) for a in (hidden, grad_out, weight))
    return pl.pallas_call(
        kernel,
        out_shape=(jax.ShapeDtypeStruct((T, F), BF16), jax.ShapeDtypeStruct((F, SUB), BF16)),
        in_specs=[pl.BlockSpec(memory_space=pltpu.HBM)] * 3,
        out_specs=(pl.BlockSpec(memory_space=pl.ANY), pl.BlockSpec(memory_space=pl.ANY)),
        scratch_shapes=[
            pltpu.VMEM((16, T, F), BF16),
            pltpu.VMEM((NW, TILE, M), BF16),
            pltpu.VMEM((8, U, M), BF16),
            pltpu.VMEM((8, 4, U, SUB), BF16),
            pltpu.VMEM((16, T, SUB), BF16),
            pltpu.VMEM((T, F), F32),
            pltpu.VMEM((3, T, F), BF16),
            pltpu.VMEM((2, HALF, F), BF16),
            pltpu.VMEM((2, T, F), BF16),
            pltpu.VMEM((F, SUB), F32),
            pltpu.VMEM((F, SUB), BF16),
            pltpu.VMEM((T, F), BF16),
            pltpu.SemaphoreType.DMA((64,)),
            pltpu.SemaphoreType.DMA((64,)),
            pltpu.SemaphoreType.DMA((4,)),
            pltpu.SemaphoreType.DMA((4,)),
            pltpu.SemaphoreType.DMA((4,)),
            pltpu.SemaphoreType.DMA((F // TILE,)),
            pltpu.SemaphoreType.DMA((NW,)),
        ],
        compiler_params=pltpu.CompilerParams(
            collective_id=0, has_side_effects=True, vmem_limit_bytes=42 * 2**20
        ),
        cost_estimate=pl.CostEstimate(
            flops=4 * 512 * M * F, bytes_accessed=2 * F * (M + SUB + 2 * T), transcendentals=0
        ),
    )(hidden, grad_out, weight)


def solution(mesh):
    return jax.shard_map(
        shards,
        mesh=mesh,
        in_specs=(P(("depth", "row"), "col"), P(("depth", "col"), "row"), P("col", "row")),
        out_specs=(P(("depth", "row"), "col"), P("col", ("depth", "row"))),
        check_vma=False,
    )
```

time: 87.7 us -> 82.2 us (0.937)
  local copies, waits for them, and re-layouts: 6.04 us -> 2.65 us
  Pallas kernels: 80.9 us -> 78.8 us
    unnamed x2, local copies, waits for them, and re-layouts: 6.04 us -> 2.65 us
    pallas_call x1, Pallas kernels: 80.9 us -> 78.8 us  [shards(): pl.pallas_call(kernel, out_shape=(jax.ShapeDtypeStruct((T, F), BF16), jax...]
where the time goes in v3:
time: 82.2 us; the launch traced here: 82.1 us
  Pallas kernels  78.8 us (96%)
  local copies, waits for them, and re-layouts  2.65 us (3%)
    pallas_call x1, Pallas kernels, shards(): pl.pallas_call(kernel, out_shape=(jax.ShapeDtypeStruct((T, F), BF16), jax...  78.8 us
    unnamed x2, local copies, waits for them, and re-layouts  2.65 us

profile of v3, /device:TPU:1, one launch (start us, length us, event | category | flops | bytes accessed | tf_op | source)
XLA Modules:
  0.0 82.1 jit_solution(12355161310251238021)
XLA Ops:
  0.6 78.8 %shard_map.50 = (bf16[128,3328]{1,0:T(8,128)(2,1)S(1)}, bf16[3328,512]{1,0:T(8,128)(2,1)S(1)}) custom-call(bf16[128,3328]{1,0:T(8,128)(2,1)} %h_ref.1, bf16[64,2048]{1,0:T(8,128)(2,1)} %g_ref.1, bf16[3328,2048]{1,0:T(8,128)(2,1)} %w_ref.1), custom_call_target="tpu_custom_call" | custom-call | flops 13958643712 | bytes 18743296 | tf_op jit(solution)/shard_map/pallas_call | solution.py:315
  79.5 0.9 %copy.7 = bf16[128,3328]{1,0:T(8,128)(2,1)} copy(bf16[128,3328]{1,0:T(8,128)(2,1)S(1)} %get-tuple-element.4) | data formatting | bytes 1703936
  80.4 1.7 %copy.8 = bf16[3328,512]{1,0:T(8,128)(2,1)} copy(bf16[3328,512]{1,0:T(8,128)(2,1)S(1)} %get-tuple-element.5) | data formatting | bytes 6815744

commit v4 on v3

--- a/solution.py
+++ b/solution.py
@@ -29,8 +29,8 @@
 
 def kernel(
     h_ref, g_ref, w_ref, hg_ref, dw_ref,
-    hb, wv, g1, st, g2, own, pb, r1, r2, acc, dwv, hgv,
-    ssem, rsem, a2s, a2r, lsem, osem, wsem,
+    hb, wv, g1, st, g2, own, pb, r1, r2, acc,
+    ssem, rsem, a2s, a2r, lsem, wsem,
 ):
     d, r, c = lax.axis_index("depth"), lax.axis_index("row"), lax.axis_index("col")
     zl, k, zh, y = d // 2, d % 2, c // 4, c % 4
@@ -82,6 +82,13 @@
         )
         cp.start()
         copies[key] = cp
+
+    done = []
+
+    def sent(n):
+        for cp in list(copies.values())[len(done) : n]:
+            cp.wait_send()
+            done.append(cp)
 
     def got(*keys):
         for key in keys:
@@ -196,6 +203,7 @@
     pl.loop(7, F // TILE)(feature_sums)
 
     lo, hi = pl.ds(0, HALF), pl.ds(HALF, HALF)
+    early = len(copies)
     send("r1lo", pb.at[1, lo], r1.at[0], xm)
     send("r1hi", pb.at[1, hi], r1.at[1], xp)
     send("r2alo", pb.at[0, lo], r2.at[0, lo], xp)
@@ -255,6 +263,14 @@
     for dx in (3, 1):
         got(("z", slot(1, 0, dx), ALO), ("z", slot(1, 0, dx), AHI))
         pass_on("s", sib, slot(1, 0, dx), slot(1, 1, dx), (0, T))
+
+    sent(early)
+    for i in range(1, 4):
+        a2a[i].wait_send()
+
+    @pl.when(jnp.logical_not(same))
+    def _():
+        a2a[0].wait_send()
 
     for dx in (1, 3):
         got(("s", slot(1, 1, dx), (0, T)))
@@ -280,34 +296,16 @@
         @pl.loop(cols[0] // TILE, cols[1] // TILE)
         def _(n):
             at = pl.ds(pl.multiple_of(n * TILE, TILE), TILE)
-            dwv[at, :] = ((acc[at, :] + product(14, 16, at)) * SCALE).astype(BF16)
-            pltpu.make_async_copy(dwv.at[at], dw_ref.at[at], osem.at[n]).start()
+            dw_ref[at, :] = ((acc[at, :] + product(14, 16, at)) * SCALE).astype(BF16)
 
     got("r2alo", "r2bhi")
     own[lo, :] += r2[0, lo, :].astype(F32)
     own[hi, :] += r2[1, hi, :].astype(F32)
-    hg_copies = []
     for i, (name, half) in enumerate((("r2blo", lo), ("r2ahi", hi))):
         got(name)
-        hgv[half, :] = (own[half, :] + r2[1 - i, half, :].astype(F32)).astype(BF16)
-        hg_copies.append(pltpu.make_async_copy(hgv.at[half], hg_ref.at[half], lsem.at[2 + i]))
-        hg_copies[i].start()
-
-    @pl.loop(0, F // TILE)
-    def _(n):
-        at = pl.ds(pl.multiple_of(n * TILE, TILE), TILE)
-        pltpu.make_async_copy(dwv.at[at], dw_ref.at[at], osem.at[n]).wait()
-
-    for cp in hg_copies:
-        cp.wait()
-    for cp in copies.values():
-        cp.wait_send()
-    for i in range(1, 4):
-        a2a[i].wait_send()
-
-    @pl.when(jnp.logical_not(same))
-    def _():
-        a2a[0].wait_send()
+        hg_ref[half, :] = (own[half, :] + r2[1 - i, half, :].astype(F32)).astype(BF16)
+
+    sent(len(copies))
 
 
 def shards(hidden, grad_out, weight):
@@ -316,7 +314,7 @@
         kernel,
         out_shape=(jax.ShapeDtypeStruct((T, F), BF16), jax.ShapeDtypeStruct((F, SUB), BF16)),
         in_specs=[pl.BlockSpec(memory_space=pltpu.HBM)] * 3,
-        out_specs=(pl.BlockSpec(memory_space=pl.ANY), pl.BlockSpec(memory_space=pl.ANY)),
+        out_specs=(pl.BlockSpec(memory_space=pltpu.VMEM), pl.BlockSpec(memory_space=pltpu.VMEM)),
         scratch_shapes=[
             pltpu.VMEM((16, T, F), BF16),
             pltpu.VMEM((NW, TILE, M), BF16),
@@ -328,18 +326,15 @@
             pltpu.VMEM((2, HALF, F), BF16),
             pltpu.VMEM((2, T, F), BF16),
             pltpu.VMEM((F, SUB), F32),
-            pltpu.VMEM((F, SUB), BF16),
-            pltpu.VMEM((T, F), BF16),
             pltpu.SemaphoreType.DMA((64,)),
             pltpu.SemaphoreType.DMA((64,)),
             pltpu.SemaphoreType.DMA((4,)),
             pltpu.SemaphoreType.DMA((4,)),
-            pltpu.SemaphoreType.DMA((4,)),
-            pltpu.SemaphoreType.DMA((F // TILE,)),
+            pltpu.SemaphoreType.DMA((2,)),
             pltpu.SemaphoreType.DMA((NW,)),
         ],
         compiler_params=pltpu.CompilerParams(
-            collective_id=0, has_side_effects=True, vmem_limit_bytes=42 * 2**20
+            collective_id=0, has_side_effects=True, vmem_limit_bytes=44 * 2**20
         ),
         cost_estimate=pl.CostEstimate(
             flops=4 * 512 * M * F, bytes_accessed=2 * F * (M + SUB + 2 * T), transcendentals=0

time: 82.2 us -> 81.3 us (0.989)
  Pallas kernels: 78.8 us -> 77.9 us
    pallas_call x1, Pallas kernels: 78.8 us -> 77.9 us  [shards(): pl.pallas_call(kernel, out_shape=(jax.ShapeDtypeStruct((T, F), BF16), jax...]
where the time goes in v4:
time: 81.3 us; the launch traced here: 81.2 us
  Pallas kernels  77.9 us (96%)
  local copies, waits for them, and re-layouts  2.65 us (3%)
    pallas_call x1, Pallas kernels, shards(): pl.pallas_call(kernel, out_shape=(jax.ShapeDtypeStruct((T, F), BF16), jax...  77.9 us
    unnamed x2, local copies, waits for them, and re-layouts  2.65 us

profile of v4, /device:TPU:1, one launch (start us, length us, event | category | flops | bytes accessed | tf_op | source)
XLA Modules:
  0.0 81.2 jit_solution(17597749012793744634)
XLA Ops:
  0.6 77.9 %shard_map.50 = (bf16[128,3328]{1,0:T(8,128)(2,1)S(1)}, bf16[3328,512]{1,0:T(8,128)(2,1)S(1)}) custom-call(bf16[128,3328]{1,0:T(8,128)(2,1)} %h_ref.1, bf16[64,2048]{1,0:T(8,128)(2,1)} %g_ref.1, bf16[3328,2048]{1,0:T(8,128)(2,1)} %w_ref.1), custom_call_target="tpu_custom_call" | custom-call | flops 13958643712 | bytes 18743296 | tf_op jit(solution)/shard_map/pallas_call | solution.py:313
  78.5 0.9 %copy.7 = bf16[128,3328]{1,0:T(8,128)(2,1)} copy(bf16[128,3328]{1,0:T(8,128)(2,1)S(1)} %get-tuple-element.4) | data formatting | bytes 1703936
  79.4 1.7 %copy.8 = bf16[3328,512]{1,0:T(8,128)(2,1)} copy(bf16[3328,512]{1,0:T(8,128)(2,1)S(1)} %get-tuple-element.5) | data formatting | bytes 6815744

commit v5 on v4

--- a/solution.py
+++ b/solution.py
@@ -290,6 +290,10 @@
             pass_on("s", sib, s, slot(1, 1, 2), part, cols)
         if cols == COLS[0]:
             got(("s", slot(1, 1, 2), BLO), ("s", slot(1, 1, 2), BHI))
+        if cols == COLS[1]:
+            got("r2alo", "r2bhi")
+            own[lo, :] += r2[0, lo, :].astype(F32)
+            own[hi, :] += r2[1, hi, :].astype(F32)
         for part in (ALO, AHI):
             got(("s", slot(1, 1, 2), part, cols))
 
@@ -298,9 +302,6 @@
             at = pl.ds(pl.multiple_of(n * TILE, TILE), TILE)
             dw_ref[at, :] = ((acc[at, :] + product(14, 16, at)) * SCALE).astype(BF16)
 
-    got("r2alo", "r2bhi")
-    own[lo, :] += r2[0, lo, :].astype(F32)
-    own[hi, :] += r2[1, hi, :].astype(F32)
     for i, (name, half) in enumerate((("r2blo", lo), ("r2ahi", hi))):
         got(name)
         hg_ref[half, :] = (own[half, :] + r2[1 - i, half, :].astype(F32)).astype(BF16)

time: 81.3 us -> 81.2 us (level)
  no operation moved by 1% of the time
where the time goes in v5:
time: 81.2 us; the launch traced here: 81.1 us
  Pallas kernels  77.8 us (96%)
  local copies, waits for them, and re-layouts  2.65 us (3%)
    pallas_call x1, Pallas kernels, shards(): pl.pallas_call(kernel, out_shape=(jax.ShapeDtypeStruct((T, F), BF16), jax...  77.8 us
    unnamed x2, local copies, waits for them, and re-layouts  2.65 us

profile of v5, /device:TPU:1, one launch (start us, length us, event | category | flops | bytes accessed | tf_op | source)
XLA Modules:
  0.0 81.1 jit_solution(5911076289076762546)
XLA Ops:
  0.6 77.8 %shard_map.50 = (bf16[128,3328]{1,0:T(8,128)(2,1)S(1)}, bf16[3328,512]{1,0:T(8,128)(2,1)S(1)}) custom-call(bf16[128,3328]{1,0:T(8,128)(2,1)} %h_ref.1, bf16[64,2048]{1,0:T(8,128)(2,1)} %g_ref.1, bf16[3328,2048]{1,0:T(8,128)(2,1)} %w_ref.1), custom_call_target="tpu_custom_call" | custom-call | flops 13958643712 | bytes 18743296 | tf_op jit(solution)/shard_map/pallas_call | solution.py:314
  78.4 0.9 %copy.7 = bf16[128,3328]{1,0:T(8,128)(2,1)} copy(bf16[128,3328]{1,0:T(8,128)(2,1)S(1)} %get-tuple-element.4) | data formatting | bytes 1703936
  79.3 1.7 %copy.8 = bf16[3328,512]{1,0:T(8,128)(2,1)} copy(bf16[3328,512]{1,0:T(8,128)(2,1)S(1)} %get-tuple-element.5) | data formatting | bytes 6815744

commit v6 on v5

--- a/solution.py
+++ b/solution.py
@@ -253,6 +253,7 @@
         at = pl.ds(pl.multiple_of(n * TILE, TILE), TILE)
         acc[at, :] = product(0, 10, at)
 
+    middle = len(copies)
     got("r1lo")
     pb[2, lo, :] = (pb[2, lo, :].astype(F32) + r1[0].astype(F32)).astype(BF16)
     send("r2blo", pb.at[2, lo], r2.at[1, lo], xm)
@@ -294,6 +295,7 @@
             got("r2alo", "r2bhi")
             own[lo, :] += r2[0, lo, :].astype(F32)
             own[hi, :] += r2[1, hi, :].astype(F32)
+            sent(middle)
         for part in (ALO, AHI):
             got(("s", slot(1, 1, 2), part, cols))
 

time: 81.2 us -> 81.1 us (level)
  no operation moved by 1% of the time
where the time goes in v6:
time: 81.1 us; the launch traced here: 81 us
  Pallas kernels  77.7 us (96%)
  local copies, waits for them, and re-layouts  2.65 us (3%)
    pallas_call x1, Pallas kernels, shards(): pl.pallas_call(kernel, out_shape=(jax.ShapeDtypeStruct((T, F), BF16), jax...  77.7 us
    unnamed x2, local copies, waits for them, and re-layouts  2.65 us

profile of v6, /device:TPU:1, one launch (start us, length us, event | category | flops | bytes accessed | tf_op | source)
XLA Modules:
  0.0 81.0 jit_solution(14155959675007759295)
XLA Ops:
  0.6 77.7 %shard_map.50 = (bf16[128,3328]{1,0:T(8,128)(2,1)S(1)}, bf16[3328,512]{1,0:T(8,128)(2,1)S(1)}) custom-call(bf16[128,3328]{1,0:T(8,128)(2,1)} %h_ref.1, bf16[64,2048]{1,0:T(8,128)(2,1)} %g_ref.1, bf16[3328,2048]{1,0:T(8,128)(2,1)} %w_ref.1), custom_call_target="tpu_custom_call" | custom-call | flops 13958643712 | bytes 18743296 | tf_op jit(solution)/shard_map/pallas_call | solution.py:316
  78.4 0.9 %copy.7 = bf16[128,3328]{1,0:T(8,128)(2,1)} copy(bf16[128,3328]{1,0:T(8,128)(2,1)S(1)} %get-tuple-element.4) | data formatting | bytes 1703936
  79.3 1.7 %copy.8 = bf16[3328,512]{1,0:T(8,128)(2,1)} copy(bf16[3328,512]{1,0:T(8,128)(2,1)S(1)} %get-tuple-element.5) | data formatting | bytes 6815744
